TPU v7x, 512 devices: a whole 4x4x16 slice. The times are simulated.
512 devices in a mesh: vocab: 32 (over x, y, core), dp: 16 (over z).
Axes of the slice: x: 4, y: 4, z: 16, core: 2. Of those that a mesh axis runs over, the one named last changes fastest.
Arguments:
- hidden: bfloat16 [2048, 2048], P('dp', 'vocab')
- head_weight: bfloat16 [2048, 65536], P('dp', 'vocab')
- teacher_logits: bfloat16 [2048, 65536], P('dp', 'vocab')
- target_ids: int32 [2048], P('dp'), may hold values from 0 to 65535
- segment_ids: int32 [16, 128], P('dp'), may hold values from 0 to 15, never falling along the last dimension, each value on 1 to 16 neighbouring positions
- pair_order: int32 [16, 16], P('dp'), may hold values from 0 to 15, each once within a row
Outputs:
- hidden_grad: bfloat16 [2048, 2048], P('dp', 'vocab')
- head_grad: float32 [2048, 65536], P('dp', 'vocab')
- loss: float32 [], replicated
Inputs may be any that keep to these rules, and one draw needn't show every extreme that they name: `segment_ids`: in each group the row's sequence number never falls along the rows, and every sequence has 1 to 16 rows. `pair_order`: each group's row is a permutation of its 16 sequences; pair p is entry 2p (chosen) and entry 2p + 1 (rejected).
All inputs are finite; a program needn't handle non-finite values.
Results may differ from a plain program's by a relative error of at most 0.018.
Values may be sent and summed in bfloat16 or wider, within the bound.
No kernel may reach another device: no remote copies, remote signals or barrier semaphores. Data moves between devices by JAX's collectives and lax.ppermute only.
A program may use at most 64 MiB of HBM per device.

v0:
```python
import jax
import jax.numpy as jnp
from jax import lax
from jax.sharding import PartitionSpec as P

dpo_beta = 0.1
dpo_gamma = 4.0


def pair_weights(log_ratio, segments, ordering):
    seq_count = ordering.shape[0]
    labels = lax.broadcasted_iota(jnp.int32, (1, seq_count), 1)
    seq_hot = (segments[:, None] == labels).astype(jnp.float32)
    seq_ratio = jnp.sum(seq_hot * log_ratio[:, None], axis=0)
    chosen = ordering[0::2]
    rejected = ordering[1::2]
    chosen_hot = (chosen[:, None] == labels).astype(jnp.float32)
    rejected_hot = (rejected[:, None] == labels).astype(jnp.float32)
    margin = dpo_beta * (
        jnp.sum(chosen_hot * seq_ratio[None, :], axis=1)
        - jnp.sum(rejected_hot * seq_ratio[None, :], axis=1)
    )
    strength = dpo_gamma * dpo_beta * jax.nn.sigmoid(-margin)
    coeffs = jnp.sum((rejected_hot - chosen_hot) * strength[:, None], axis=0)
    row_weight = jnp.sum(seq_hot * coeffs[None, :], axis=1)
    return (row_weight, jnp.sum(jax.nn.softplus(-margin)))


def to_all(block, axis):
    count = lax.axis_size(axis)
    copies = jnp.broadcast_to(block[None], (count,) + block.shape)
    return lax.all_to_all(copies, axis, 0, 0, tiled=True)


def on_device(hidden, head_weight, teacher_logits, target_ids, segment_ids, pair_order):
    f32, bf16 = (jnp.float32, jnp.bfloat16)
    rows_full = lax.all_gather(hidden, "vocab", axis=1, tiled=True)
    width = head_weight.shape[1]
    half = width // 2
    weight_lo = lax.all_gather(head_weight[:, :half], "dp", axis=0, tiled=True)
    weight_hi = lax.all_gather(head_weight[:, half:], "dp", axis=0, tiled=True)
    student = jnp.concatenate(
        [
            jnp.dot(rows_full, weight_lo, preferred_element_type=f32),
            jnp.dot(rows_full, weight_hi, preferred_element_type=f32),
        ],
        axis=1,
    )
    teacher = teacher_logits.astype(f32)
    n_vocab = lax.axis_size("vocab")
    n_dp = lax.axis_size("dp")
    rows = student.shape[0]
    offset = lax.axis_index("vocab") * width
    column = lax.broadcasted_iota(jnp.int32, student.shape, 1) + offset
    is_target = column == target_ids[:, None]
    own_max = jnp.max(student, axis=1)
    own_tmax = jnp.max(teacher, axis=1)
    own_exp = jnp.exp(student - own_max[:, None])
    own_texp = jnp.exp(teacher - own_tmax[:, None])
    stats = jnp.stack(
        [
            own_max,
            own_tmax,
            jnp.sum(own_exp, axis=1),
            jnp.sum(own_texp, axis=1),
            jnp.sum(own_texp * (teacher - student), axis=1),
            jnp.sum(jnp.where(is_target, student, 0.0), axis=1),
            jnp.sum(jnp.where(is_target, teacher, 0.0), axis=1),
            jnp.zeros((rows,), f32),
        ]
    )
    every = to_all(stats, "vocab").reshape(n_vocab, 8, rows)
    max_student = jnp.max(every[:, 0], axis=0)
    max_teacher = jnp.max(every[:, 1], axis=0)
    scale_s = jnp.exp(every[:, 0] - max_student[None])
    scale_t = jnp.exp(every[:, 1] - max_teacher[None])
    sum_student = jnp.sum(every[:, 2] * scale_s, axis=0)
    sum_teacher = jnp.sum(every[:, 3] * scale_t, axis=0)
    cross = jnp.sum(every[:, 4] * scale_t, axis=0)
    target_student = jnp.sum(every[:, 5], axis=0)
    target_teacher = jnp.sum(every[:, 6], axis=0)
    lse_student = max_student + jnp.log(sum_student)
    lse_teacher = max_teacher + jnp.log(sum_teacher)
    kl_rows = cross / sum_teacher - lse_teacher + lse_student
    log_ratio = target_student - lse_student - (target_teacher - lse_teacher)
    row_weight, dpo_sum = pair_weights(log_ratio, segment_ids[0], pair_order[0])
    group_objective = jnp.sum(kl_rows) + dpo_gamma * dpo_sum
    exp_student = jnp.exp(student - max_student[:, None])
    exp_teacher = jnp.exp(teacher - max_teacher[:, None])
    prob_student = exp_student / sum_student[:, None]
    prob_teacher = exp_teacher / sum_teacher[:, None]
    logit_grad = (
        prob_student - prob_teacher + row_weight[:, None] * (is_target.astype(f32) - prob_student)
    ).astype(bf16)
    grad_lo = logit_grad[:, :half]
    grad_hi = logit_grad[:, half:]
    all_lo = lax.all_gather(grad_lo, "dp", axis=0, tiled=True)
    all_hi = lax.all_gather(grad_hi, "dp", axis=0, tiled=True)
    nt = (((1,), (1,)), ((), ()))
    hidden_term = (
        lax.dot_general(grad_lo, weight_lo, nt, preferred_element_type=f32)
        + lax.dot_general(grad_hi, weight_hi, nt, preferred_element_type=f32)
    ).astype(bf16)
    feats = hidden_term.shape[1] // n_vocab
    terms = hidden_term.reshape(rows, n_vocab, feats).swapaxes(0, 1)
    terms = lax.all_to_all(terms, "vocab", 0, 0, tiled=True)
    hidden_grad = jnp.sum(terms.astype(f32), axis=0).astype(bf16)
    objectives = to_all(jnp.full((8, 128), group_objective, f32), "dp").reshape(n_dp, 8, 128)
    loss_value = jnp.sum(objectives[:, 0, 0]) / (rows * n_dp)
    grad_cols = lax.all_to_all(rows_full, "dp", split_axis=1, concat_axis=0, tiled=True)
    tn = (((0,), (0,)), ((), ()))
    head_grad = jnp.concatenate(
        [
            lax.dot_general(grad_cols, all_lo, tn, preferred_element_type=f32),
            lax.dot_general(grad_cols, all_hi, tn, preferred_element_type=f32),
        ],
        axis=1,
    )
    return (hidden_grad, head_grad, loss_value)


def solution(mesh):
    return jax.shard_map(
        on_device,
        mesh=mesh,
        in_specs=(
            P("dp", "vocab"),
            P("dp", "vocab"),
            P("dp", "vocab"),
            P("dp"),
            P("dp", None),
            P("dp", None),
        ),
        out_specs=(P("dp", "vocab"), P("dp", "vocab"), P()),
        check_vma=False,
    )
```

profile of v0, /device:TPU:2, one launch (start us, length us, event | category | flops | bytes accessed | tf_op | source)
XLA Modules:
  0.0 374.6 jit_solution(1377167011678018934)
XLA Ops:
  7.2 0.0 all-gather.5.cloned.1.call-start
  7.2 1.8 fusion.19
  9.0 0.0 all-gather.5.cloned.1.call-update
  9.1 0.0 all-gather.7.cloned.1.call-start
  9.1 0.7 all-gather.7.cloned.1.call-update
  9.8 1.2 reduce_max.71
  11.0 29.9 %all_gather.15 = bf16[128,2048]{0,1:T(8,128)(2,1)} all-gather(bf16[128,64]{0,1:T(8,128)(2,1)} %param.6), channel_id=1, replica_groups=mesh['vocab'=32,'dp'=16] {'vocab'}, dimensions={1}, use_global_device_ids=true | all-gather | bytes 540672 | tf_op jit(solution)/shard_map/all_gather | solution.py:37
  40.9 52.3 %all-gather.5.cloned.1.call-done = bf16[2048,1024]{1,0:T(8,128)(2,1)} async-done(((bf16[128,1024]{1,0:T(8,128)(2,1)}), bf16[2048,1024]{1,0:T(8,128)(2,1)}) %all-gather.5.cloned.1.call-update) | async-done | bytes 4194320 | tf_op jit(solution)/shard_map/all_gather | solution.py:40
  93.3 3.2 fusion.22
  96.5 74.8 %all-gather.7.cloned.1.call-done = bf16[2048,1024]{1,0:T(8,128)(2,1)} async-done(((bf16[128,1024]{1,0:T(8,128)(2,1)}), bf16[2048,1024]{1,0:T(8,128)(2,1)}) %all-gather.7.cloned.1.call-update) | async-done | bytes 4194320 | tf_op jit(solution)/shard_map/all_gather | solution.py:41
  171.3 3.2 fusion.23
  174.5 0.8 fusion.1
  175.4 0.7 broadcast_in_dim.8
  176.0 7.4 %all-to-all-start = ((f32[32,8,128]{2,1,0:T(8,128)}), f32[32,8,128]{2,1,0:T(8,128)S(1)}, u32[]{:S(2)}, u32[]{:S(2)}) async-start(f32[32,8,128]{2,1,0:T(8,128)} %broadcast_in_dim.8), calls=%async_computation | async-start | bytes 262144 | tf_op jit(solution)/shard_map/all_to_all | solution.py:32
  183.5 0.0 all-gather.9.cloned.1.call-start
  183.5 0.1 slice.51
  183.6 0.1 slice.50
  183.7 6.4 %all-to-all-done = f32[32,8,128]{2,1,0:T(8,128)S(1)} async-done(((f32[32,8,128]{2,1,0:T(8,128)}), f32[32,8,128]{2,1,0:T(8,128)S(1)}, u32[]{:S(2)}, u32[]{:S(2)}) %all-to-all-start) | async-done | bytes 131104 | tf_op jit(solution)/shard_map/all_to_all | solution.py:32
  190.1 0.1 fusion.20
  190.3 0.6 add_reduce_fusion
  190.9 0.1 select_reduce_fusion.1
  191.0 0.2 select_reduce_fusion.2
  191.3 0.6 fusion.14
  191.9 0.1 multiply_reduce_fusion.3
  192.0 0.1 select_reduce_fusion
  192.1 0.6 fusion.5
  192.7 0.9 fusion.18
  193.6 0.0 all-gather.11.cloned.1.call-start
  193.6 0.5 all-gather.11.cloned.1.call-update
  194.1 7.4 %all-to-all-start.2 = ((bf16[128,16,128]{0,2,1:T(8,128)(2,1)}), bf16[128,16,128]{0,2,1:T(8,128)(2,1)S(1)}, u32[]{:S(2)}, u32[]{:S(2)}) async-start(bf16[128,16,128]{0,2,1:T(8,128)(2,1)} %bitcast.17), calls=%async_computation.2 | async-start | bytes 1048576 | tf_op jit(solution)/shard_map/all_to_all | solution.py:110
  202.9 3.8 %fusion.16 = f32[128,2048]{1,0:T(8,128)S(1)} fusion(bf16[2048,1024]{1,0:T(8,128)(2,1)} %all-gather.5.cloned.1.call-done, bf16[128,2048]{1,0:T(8,128)(2,1)S(1)} %fusion.5), kind=kOutput, calls=%fused_computation.50 | convolution fusion | flops 536870912 | bytes 5505024 | tf_op jit(solution)/shard_map/dot_general | solution.py:101
  206.7 29.5 %all-to-all-done.2 = bf16[128,16,128]{0,2,1:T(8,128)(2,1)S(1)} async-done(((bf16[128,16,128]{0,2,1:T(8,128)(2,1)}), bf16[128,16,128]{0,2,1:T(8,128)(2,1)S(1)}, u32[]{:S(2)}, u32[]{:S(2)}) %all-to-all-start.2) | async-done | bytes 524320 | tf_op jit(solution)/shard_map/all_to_all | solution.py:110
  236.2 0.6 broadcast_in_dim_broadcast_in_dim_broadcast_in_dim.3
  236.8 6.4 %all-to-all-start.3 = ((f32[16,8,128]{2,1,0:T(8,128)}), f32[16,8,128]{2,1,0:T(8,128)S(1)}, u32[]{:S(2)}, u32[]{:S(2)}) async-start(f32[16,8,128]{2,1,0:T(8,128)} %broadcast_in_dim_broadcast_in_dim_broadcast_in_dim.3), calls=%async_computation.3 | async-start | bytes 131072 | tf_op jit(solution)/shard_map/all_to_all | solution.py:32
  243.2 3.7 fusion
  246.9 1.0 copy.32
  247.9 8.8 %all-to-all-done.3 = f32[16,8,128]{2,1,0:T(8,128)S(1)} async-done(((f32[16,8,128]{2,1,0:T(8,128)}), f32[16,8,128]{2,1,0:T(8,128)S(1)}, u32[]{:S(2)}, u32[]{:S(2)}) %all-to-all-start.3) | async-done | bytes 65568 | tf_op jit(solution)/shard_map/all_to_all | solution.py:32
  256.8 5.0 %all-to-all-start.1 = ((bf16[32,128,64]{1,2,0:T(8,128)(2,1)}), bf16[32,128,64]{1,2,0:T(8,128)(2,1)S(1)}, u32[]{:S(2)}, u32[]{:S(2)}) async-start(bf16[32,128,64]{1,2,0:T(8,128)(2,1)} %bitcast.16), calls=%async_computation.1 | async-start | bytes 1048576 | tf_op jit(solution)/shard_map/all_to_all | solution.py:106
  261.8 0.3 copy.33
  262.1 0.6 slice_reduce_fusion
  263.4 8.2 %all-to-all-done.1 = bf16[32,128,64]{1,2,0:T(8,128)(2,1)S(1)} async-done(((bf16[32,128,64]{1,2,0:T(8,128)(2,1)}), bf16[32,128,64]{1,2,0:T(8,128)(2,1)S(1)}, u32[]{:S(2)}, u32[]{:S(2)}) %all-to-all-start.1) | async-done | bytes 524320 | tf_op jit(solution)/shard_map/all_to_all | solution.py:106
  271.5 0.7 reduce_sum.188
  272.2 15.8 %all-gather.9.cloned.1.call-done = bf16[2048,1024]{1,0:T(8,128)(2,1)} async-done(((bf16[128,1024]{1,0:T(8,128)(2,1)}), bf16[2048,1024]{1,0:T(8,128)(2,1)}) %all-gather.9.cloned.1.call-update) | async-done | bytes 4194320 | tf_op jit(solution)/shard_map/all_gather | solution.py:97
  288.0 3.5 convolution_bitcast_fusion.1
  291.5 70.6 %all-gather.11.cloned.1.call-done = bf16[2048,1024]{1,0:T(8,128)(2,1)} async-done(((bf16[128,1024]{1,0:T(8,128)(2,1)}), bf16[2048,1024]{1,0:T(8,128)(2,1)}) %all-gather.11.cloned.1.call-update) | async-done | bytes 4194320 | tf_op jit(solution)/shard_map/all_gather | solution.py:98
  362.1 3.5 convolution_bitcast_fusion
  365.5 0.1 pad_maximum_fusion.1
  365.6 1.3 copy.35
  (19 shorter events, 0.2 us)
Async XLA Ops:
  7.2 86.1 %all-gather.5.cloned.1.call-start = ((), (), s32[]{:S(2)}) async-start(), calls=%async_computation.4 | async-start | bytes 4456448 | tf_op jit(solution)/shard_map/all_gather | solution.py:40
  9.1 162.2 %all-gather.7.cloned.1.call-start = ((), (), s32[]{:S(2)}) async-start(), calls=%async_computation.5 | async-start | bytes 4456448 | tf_op jit(solution)/shard_map/all_gather | solution.py:41
  40.9 133.6 %copy-start = (bf16[128,2048]{1,0:T(8,128)(2,1)S(1)}, bf16[128,2048]{1,0:T(8,128)(2,1)}, u32[]{:S(2)}) copy-start(bf16[128,2048]{1,0:T(8,128)(2,1)} %param.8) | copy-start | bytes 1572868
  40.9 133.6 %copy-start.1 = (s32[128]{0:T(128)S(1)}, s32[128]{0:T(128)}, u32[]{:S(2)}) copy-start(s32[128]{0:T(128)} %param.9) | copy-start | bytes 1540
  96.4 87.1 %copy-start.2 = (s32[1,16]{1,0:T(1,128)S(1)}, s32[1,16]{1,0:T(1,128)}, u32[]{:S(2)}) copy-start(s32[1,16]{1,0:T(1,128)} %param.11) | copy-start | bytes 196
  96.5 94.5 %copy-start.3 = (s32[1,128]{1,0:T(1,128)S(1)}, s32[1,128]{1,0:T(1,128)}, u32[]{:S(2)}) copy-start(s32[1,128]{1,0:T(1,128)} %param.10) | copy-start | bytes 1540
  176.0 14.1 %all-to-all-start = ((f32[32,8,128]{2,1,0:T(8,128)}), f32[32,8,128]{2,1,0:T(8,128)S(1)}, u32[]{:S(2)}, u32[]{:S(2)}) async-start(f32[32,8,128]{2,1,0:T(8,128)} %broadcast_in_dim.8), calls=%async_computation | async-start | bytes 262144 | tf_op jit(solution)/shard_map/all_to_all | solution.py:32
  183.5 104.5 %all-gather.9.cloned.1.call-start = ((), (), s32[]{:S(2)}) async-start(), calls=%async_computation.6 | async-start | bytes 4456448 | tf_op jit(solution)/shard_map/all_gather | solution.py:97
  193.6 168.5 %all-gather.11.cloned.1.call-start = ((), (), s32[]{:S(2)}) async-start(), calls=%async_computation.7 | async-start | bytes 4456448 | tf_op jit(solution)/shard_map/all_gather | solution.py:98
  194.1 42.0 %all-to-all-start.2 = ((bf16[128,16,128]{0,2,1:T(8,128)(2,1)}), bf16[128,16,128]{0,2,1:T(8,128)(2,1)S(1)}, u32[]{:S(2)}, u32[]{:S(2)}) async-start(bf16[128,16,128]{0,2,1:T(8,128)(2,1)} %bitcast.17), calls=%async_computation.2 | async-start | bytes 1048576 | tf_op jit(solution)/shard_map/all_to_all | solution.py:110
  236.8 20.0 %all-to-all-start.3 = ((f32[16,8,128]{2,1,0:T(8,128)}), f32[16,8,128]{2,1,0:T(8,128)S(1)}, u32[]{:S(2)}, u32[]{:S(2)}) async-start(f32[16,8,128]{2,1,0:T(8,128)} %broadcast_in_dim_broadcast_in_dim_broadcast_in_dim.3), calls=%async_computation.3 | async-start | bytes 131072 | tf_op jit(solution)/shard_map/all_to_all | solution.py:32
  256.8 14.8 %all-to-all-start.1 = ((bf16[32,128,64]{1,2,0:T(8,128)(2,1)}), bf16[32,128,64]{1,2,0:T(8,128)(2,1)S(1)}, u32[]{:S(2)}, u32[]{:S(2)}) async-start(bf16[32,128,64]{1,2,0:T(8,128)(2,1)} %bitcast.16), calls=%async_computation.1 | async-start | bytes 1048576 | tf_op jit(solution)/shard_map/all_to_all | solution.py:106
Sparse Core Ops, SparseCore 0:
  10.1 83.1 all-gather.4
  95.9 75.3 all-gather.6
  193.7 94.2 all-gather.8
  289.9 72.1 all-gather.10
where the time goes:
time: 375 us
  waiting for transfers between devices  268 us (71%)
  blocking collectives  29.9 us (8%)
  starting transfers between devices  26.5 us (7%)
  matrix products  20.8 us (6%)
  between operations  17 us (5%)
  local copies, waits for them, and re-layouts  6.89 us (2%)
  other arithmetic  5.88 us (2%)
    all_gather x1, waiting for transfers between devices, on_device(): weight_hi = lax.all_gather(head_weight[:, half:], 'dp', axis=0, tiled=True)  74.8 us
    all_gather x1, waiting for transfers between devices, on_device(): all_hi = lax.all_gather(grad_hi, 'dp', axis=0, tiled=True)  70.6 us
    all_gather x1, waiting for transfers between devices, on_device(): weight_lo = lax.all_gather(head_weight[:, :half], 'dp', axis=0, tiled=True)  52.3 us
    all_gather x1, blocking collectives, on_device(): rows_full = lax.all_gather(hidden, 'vocab', axis=1, tiled=True)  29.9 us
    all_to_all x1, waiting for transfers between devices, on_device(): lax.all_to_all(rows_full, 'dp', split_axis=1, concat_axis=0, tiled=True)  29.5 us
    all_gather x1, waiting for transfers between devices, on_device(): all_lo = lax.all_gather(grad_lo, 'dp', axis=0, tiled=True)  15.8 us
    all_to_all x2, waiting for transfers between devices, to_all(): return lax.all_to_all(copies, axis, 0, 0, tiled=True)  15.2 us
    all_to_all x2, starting transfers between devices, to_all(): return lax.all_to_all(copies, axis, 0, 0, tiled=True)  13.8 us
  transfers between devices with their start and end apart: 8, of which 8 were waited for; matrix products, arithmetic and copies ran while one was open for 5% of the time, Pallas kernels for 0%

commit v1 on v0

--- a/solution.py
+++ b/solution.py
@@ -107,7 +107,10 @@
     hidden_grad = jnp.sum(terms.astype(f32), axis=0).astype(bf16)
     objectives = to_all(jnp.full((8, 128), group_objective, f32), "dp").reshape(n_dp, 8, 128)
     loss_value = jnp.sum(objectives[:, 0, 0]) / (rows * n_dp)
-    grad_cols = lax.all_to_all(rows_full, "dp", split_axis=1, concat_axis=0, tiled=True)
+    size = lax.axis_size("dp")
+    blocks = jnp.stack(jnp.split(rows_full, size, axis=1), axis=0)
+    blocks = lax.all_to_all(blocks, "dp", split_axis=0, concat_axis=0)
+    grad_cols = jnp.concatenate(blocks, axis=0)
     tn = (((0,), (0,)), ((), ()))
     head_grad = jnp.concatenate(
         [

time: 375 us -> 379 us (1.011)
  the two profiles are of different devices: /device:TPU:2 before, /device:TPU:4 now
where the time goes in v1:
time: 379 us; the launch traced here: 378 us
  waiting for transfers between devices  268 us (71%)
  blocking collectives  26.3 us (7%)
  starting transfers between devices  25.9 us (7%)
  matrix products  17.2 us (5%)
  between operations  17.1 us (5%)
  local copies, waits for them, and re-layouts  17 us (4%)
  other arithmetic  6.86 us (2%)
    all_gather x1, waiting for transfers between devices, on_device(): weight_hi = lax.all_gather(head_weight[:, half:], 'dp', axis=0, tiled=True)  74.9 us
    all_gather x1, waiting for transfers between devices, on_device(): all_hi = lax.all_gather(grad_hi, 'dp', axis=0, tiled=True)  74.4 us
    all_gather x1, waiting for transfers between devices, on_device(): weight_lo = lax.all_gather(head_weight[:, :half], 'dp', axis=0, tiled=True)  56 us
    all_to_all x1, waiting for transfers between devices, on_device(): blocks = lax.all_to_all(blocks, 'dp', split_axis=0, concat_axis=0)  32.5 us
    all_gather x1, blocking collectives, on_device(): rows_full = lax.all_gather(hidden, 'vocab', axis=1, tiled=True)  26.3 us
    all_to_all x2, starting transfers between devices, to_all(): return lax.all_to_all(copies, axis, 0, 0, tiled=True)  14.8 us
    all_to_all x2, waiting for transfers between devices, to_all(): return lax.all_to_all(copies, axis, 0, 0, tiled=True)  12.6 us
    unnamed x41, local copies, waits for them, and re-layouts  11 us
  transfers between devices with their start and end apart: 8, of which 8 were waited for; matrix products, arithmetic and copies ran while one was open for 7% of the time, Pallas kernels for 0%

profile of v1, /device:TPU:4, one launch (start us, length us, event | category | flops | bytes accessed | tf_op | source)
XLA Modules:
  0.0 378.1 jit_solution(13991686635389292842)
XLA Ops:
  7.2 1.8 fusion.20
  9.1 0.7 all-gather.7.cloned.1.call-update
  9.8 1.2 reduce_max.71
  11.0 26.3 %all_gather.15 = bf16[128,2048]{0,1:T(8,128)(2,1)S(1)} all-gather(bf16[128,64]{0,1:T(8,128)(2,1)} %param.6), channel_id=1, replica_groups=mesh['vocab'=32,'dp'=16] {'vocab'}, dimensions={1}, use_global_device_ids=true | all-gather | bytes 540672 | tf_op jit(solution)/shard_map/all_gather | solution.py:37
  37.3 56.0 %all-gather.5.cloned.1.call-done = bf16[2048,1024]{1,0:T(8,128)(2,1)} async-done(((bf16[128,1024]{1,0:T(8,128)(2,1)}), bf16[2048,1024]{1,0:T(8,128)(2,1)}) %all-gather.5.cloned.1.call-update) | async-done | bytes 4194320 | tf_op jit(solution)/shard_map/all_gather | solution.py:40
  93.3 3.0 fusion.23
  96.4 74.9 %all-gather.7.cloned.1.call-done = bf16[2048,1024]{1,0:T(8,128)(2,1)} async-done(((bf16[128,1024]{1,0:T(8,128)(2,1)}), bf16[2048,1024]{1,0:T(8,128)(2,1)}) %all-gather.7.cloned.1.call-update) | async-done | bytes 4194320 | tf_op jit(solution)/shard_map/all_gather | solution.py:41
  171.3 3.0 fusion.24
  174.3 0.8 fusion.1
  175.2 0.7 broadcast_in_dim.8
  175.9 7.4 %all-to-all-start = ((f32[32,8,128]{2,1,0:T(8,128)}), f32[32,8,128]{2,1,0:T(8,128)S(1)}, u32[]{:S(2)}, u32[]{:S(2)}) async-start(f32[32,8,128]{2,1,0:T(8,128)} %broadcast_in_dim.8), calls=%async_computation | async-start | bytes 262144 | tf_op jit(solution)/shard_map/all_to_all | solution.py:32
  183.5 5.6 %all-to-all-done = f32[32,8,128]{2,1,0:T(8,128)S(1)} async-done(((f32[32,8,128]{2,1,0:T(8,128)}), f32[32,8,128]{2,1,0:T(8,128)S(1)}, u32[]{:S(2)}, u32[]{:S(2)}) %all-to-all-start) | async-done | bytes 131104 | tf_op jit(solution)/shard_map/all_to_all | solution.py:32
  189.3 0.6 add_reduce_fusion
  190.2 0.6 fusion.14
  191.1 0.6 fusion.5
  191.7 0.9 fusion.18
  194.9 0.6 constant_dynamic-update-slice_fusion.15
  195.6 0.6 constant_dynamic-update-slice_fusion.14
  196.2 0.6 constant_dynamic-update-slice_fusion.13
  196.8 0.6 constant_dynamic-update-slice_fusion.12
  197.4 0.6 constant_dynamic-update-slice_fusion.11
  198.0 0.6 constant_dynamic-update-slice_fusion.10
  198.6 0.6 constant_dynamic-update-slice_fusion.9
  199.2 0.6 constant_dynamic-update-slice_fusion.8
  199.8 0.6 constant_dynamic-update-slice_fusion.7
  200.4 0.6 constant_dynamic-update-slice_fusion.6
  201.0 0.6 constant_dynamic-update-slice_fusion.5
  201.6 0.6 constant_dynamic-update-slice_fusion.4
  204.1 0.6 broadcast_in_dim_broadcast_in_dim_broadcast_in_dim.3
  204.8 7.4 %all-to-all-start.3 = ((f32[16,8,128]{2,1,0:T(8,128)}), f32[16,8,128]{2,1,0:T(8,128)S(1)}, u32[]{:S(2)}, u32[]{:S(2)}) async-start(f32[16,8,128]{2,1,0:T(8,128)} %broadcast_in_dim_broadcast_in_dim_broadcast_in_dim.3), calls=%async_computation.3 | async-start | bytes 131072 | tf_op jit(solution)/shard_map/all_to_all | solution.py:32
  212.2 3.9 %fusion.16 = f32[128,2048]{1,0:T(8,128)S(1)} fusion(bf16[2048,1024]{1,0:T(8,128)(2,1)} %all-gather.5.cloned.1.call-done, bf16[128,2048]{1,0:T(8,128)(2,1)S(1)} %fusion.5), kind=kOutput, calls=%fused_computation.64 | convolution fusion | flops 536870912 | bytes 5505024 | tf_op jit(solution)/shard_map/dot_general | solution.py:101
  216.1 1.5 fusion
  217.6 1.0 copy.59
  218.6 7.0 %all-to-all-done.3 = f32[16,8,128]{2,1,0:T(8,128)S(1)} async-done(((f32[16,8,128]{2,1,0:T(8,128)}), f32[16,8,128]{2,1,0:T(8,128)S(1)}, u32[]{:S(2)}, u32[]{:S(2)}) %all-to-all-start.3) | async-done | bytes 65568 | tf_op jit(solution)/shard_map/all_to_all | solution.py:32
  225.6 6.0 %all-to-all-start.1 = ((bf16[32,128,64]{1,2,0:T(8,128)(2,1)}), bf16[32,128,64]{1,2,0:T(8,128)(2,1)S(1)}, u32[]{:S(2)}, u32[]{:S(2)}) async-start(bf16[32,128,64]{1,2,0:T(8,128)(2,1)} %bitcast.16), calls=%async_computation.1 | async-start | bytes 1048576 | tf_op jit(solution)/shard_map/all_to_all | solution.py:106
  231.6 0.6 constant_dynamic-update-slice_fusion.2
  232.5 0.6 constant_dynamic-update-slice_fusion.1
  233.1 0.6 constant_dynamic-update-slice_fusion
  233.7 7.4 %all-to-all-done.1 = bf16[32,128,64]{1,2,0:T(8,128)(2,1)S(1)} async-done(((bf16[32,128,64]{1,2,0:T(8,128)(2,1)}), bf16[32,128,64]{1,2,0:T(8,128)(2,1)S(1)}, u32[]{:S(2)}, u32[]{:S(2)}) %all-to-all-start.1) | async-done | bytes 524320 | tf_op jit(solution)/shard_map/all_to_all | solution.py:106
  241.1 4.9 %all-to-all-start.2 = ((bf16[16,128,128]{2,1,0:T(8,128)(2,1)}), bf16[16,128,128]{2,1,0:T(8,128)(2,1)S(1)}, u32[]{:S(2)}, u32[]{:S(2)}) async-start(bf16[16,128,128]{2,1,0:T(8,128)(2,1)} %constant_dynamic-update-slice_fusion), calls=%async_computation.2 | async-start | bytes 1048576 | tf_op jit(solution)/shard_map/all_to_all | solution.py:112
  246.1 0.6 slice_reduce_fusion
  247.3 0.7 reduce_sum.188
  248.0 32.5 %all-to-all-done.2 = bf16[16,128,128]{2,1,0:T(8,128)(2,1)S(1)} async-done(((bf16[16,128,128]{2,1,0:T(8,128)(2,1)}), bf16[16,128,128]{2,1,0:T(8,128)(2,1)S(1)}, u32[]{:S(2)}, u32[]{:S(2)}) %all-to-all-start.2) | async-done | bytes 524320 | tf_op jit(solution)/shard_map/all_to_all | solution.py:112
  280.5 8.6 %all-gather.9.cloned.1.call-done = bf16[2048,1024]{1,0:T(8,128)(2,1)} async-done(((bf16[128,1024]{1,0:T(8,128)(2,1)}), bf16[2048,1024]{1,0:T(8,128)(2,1)}) %all-gather.9.cloned.1.call-update) | async-done | bytes 4194320 | tf_op jit(solution)/shard_map/all_gather | solution.py:97
  289.1 2.9 fusion.25
  292.0 74.4 %all-gather.11.cloned.1.call-done = bf16[2048,1024]{1,0:T(8,128)(2,1)} async-done(((bf16[128,1024]{1,0:T(8,128)(2,1)}), bf16[2048,1024]{1,0:T(8,128)(2,1)}) %all-gather.11.cloned.1.call-update) | async-done | bytes 4194320 | tf_op jit(solution)/shard_map/all_gather | solution.py:98
  366.4 2.9 fusion.26
  369.3 1.1 pad_maximum_fusion.1
  (52 shorter events, 4.2 us)
Async XLA Ops:
  7.2 86.2 %all-gather.5.cloned.1.call-start = ((), (), s32[]{:S(2)}) async-start(), calls=%async_computation.4 | async-start | bytes 4456448 | tf_op jit(solution)/shard_map/all_gather | solution.py:40
  9.1 162.2 %all-gather.7.cloned.1.call-start = ((), (), s32[]{:S(2)}) async-start(), calls=%async_computation.5 | async-start | bytes 4456448 | tf_op jit(solution)/shard_map/all_gather | solution.py:41
  37.3 137.0 %copy-start.1 = (bf16[128,2048]{1,0:T(8,128)(2,1)S(1)}, bf16[128,2048]{1,0:T(8,128)(2,1)}, u32[]{:S(2)}) copy-start(bf16[128,2048]{1,0:T(8,128)(2,1)} %param.8) | copy-start | bytes 1572868
  37.3 137.0 %copy-start.2 = (s32[128]{0:T(128)S(1)}, s32[128]{0:T(128)}, u32[]{:S(2)}) copy-start(s32[128]{0:T(128)} %param.9) | copy-start | bytes 1540
  96.3 87.0 %copy-start.3 = (s32[1,16]{1,0:T(1,128)S(1)}, s32[1,16]{1,0:T(1,128)}, u32[]{:S(2)}) copy-start(s32[1,16]{1,0:T(1,128)} %param.11) | copy-start | bytes 196
  96.4 93.6 %copy-start.4 = (s32[1,128]{1,0:T(1,128)S(1)}, s32[1,128]{1,0:T(1,128)}, u32[]{:S(2)}) copy-start(s32[1,128]{1,0:T(1,128)} %param.10) | copy-start | bytes 1540
  175.9 13.2 %all-to-all-start = ((f32[32,8,128]{2,1,0:T(8,128)}), f32[32,8,128]{2,1,0:T(8,128)S(1)}, u32[]{:S(2)}, u32[]{:S(2)}) async-start(f32[32,8,128]{2,1,0:T(8,128)} %broadcast_in_dim.8), calls=%async_computation | async-start | bytes 262144 | tf_op jit(solution)/shard_map/all_to_all | solution.py:32
  183.3 105.8 %all-gather.9.cloned.1.call-start = ((), (), s32[]{:S(2)}) async-start(), calls=%async_computation.6 | async-start | bytes 4456448 | tf_op jit(solution)/shard_map/all_gather | solution.py:97
  192.6 173.9 %all-gather.11.cloned.1.call-start = ((), (), s32[]{:S(2)}) async-start(), calls=%async_computation.7 | async-start | bytes 4456448 | tf_op jit(solution)/shard_map/all_gather | solution.py:98
  204.8 20.8 %all-to-all-start.3 = ((f32[16,8,128]{2,1,0:T(8,128)}), f32[16,8,128]{2,1,0:T(8,128)S(1)}, u32[]{:S(2)}, u32[]{:S(2)}) async-start(f32[16,8,128]{2,1,0:T(8,128)} %broadcast_in_dim_broadcast_in_dim_broadcast_in_dim.3), calls=%async_computation.3 | async-start | bytes 131072 | tf_op jit(solution)/shard_map/all_to_all | solution.py:32
  212.2 3.9 %copy-start = (bf16[2048,1024]{1,0:T(8,128)(2,1)S(1)}, bf16[2048,1024]{1,0:T(8,128)(2,1)}, u32[]{:S(2)}) copy-start(bf16[2048,1024]{1,0:T(8,128)(2,1)} %all-gather.7.cloned.1.call-done) | copy-start | bytes 12582916
  225.6 15.5 %all-to-all-start.1 = ((bf16[32,128,64]{1,2,0:T(8,128)(2,1)}), bf16[32,128,64]{1,2,0:T(8,128)(2,1)S(1)}, u32[]{:S(2)}, u32[]{:S(2)}) async-start(bf16[32,128,64]{1,2,0:T(8,128)(2,1)} %bitcast.16), calls=%async_computation.1 | async-start | bytes 1048576 | tf_op jit(solution)/shard_map/all_to_all | solution.py:106
  241.1 39.4 %all-to-all-start.2 = ((bf16[16,128,128]{2,1,0:T(8,128)(2,1)}), bf16[16,128,128]{2,1,0:T(8,128)(2,1)S(1)}, u32[]{:S(2)}, u32[]{:S(2)}) async-start(bf16[16,128,128]{2,1,0:T(8,128)(2,1)} %constant_dynamic-update-slice_fusion), calls=%async_computation.2 | async-start | bytes 1048576 | tf_op jit(solution)/shard_map/all_to_all | solution.py:112
Sparse Core Ops, SparseCore 0:
  10.1 83.2 all-gather.4
  96.0 75.2 all-gather.6
  192.7 96.3 all-gather.8
  291.0 75.3 all-gather.10
